TPU v7x, 256 devices: a whole 4x4x8 slice. The times are simulated.
256 devices in a mesh: slab: 32 (over z, x), group: 8 (over y, core).
Axes of the slice: x: 4, y: 4, z: 8, core: 2. Of those that a mesh axis runs over, the one named last changes fastest.
Arguments:
- right_side: float32 [64, 32768], P(None, ('slab', 'group')), may hold values from -6 to 6
- fine_blocks: float32 [3, 64, 64, 32768], P(None, None, None, ('slab', 'group')), may hold values from -2 to 4
- fine_inverse: float32 [64, 64, 32768], P(None, None, ('slab', 'group')), may hold values from -0.1 to 0.6
- pattern: int32 [2, 32768], P(None, ('slab', 'group')), may hold values 0 or 1
- tentative: float32 [4, 64, 32768], P(None, None, ('slab', 'group')), may hold values from -5 to 5
- slot_map: int32 [2048, 64], P(('slab', 'group')), may hold values from 0 to 63, each once within a row
- coarse_inverse: float32 [64, 64, 2048], P(None, None, ('slab', 'group')), may hold values from -0.002 to 0.21
- coarse_lower: float32 [64, 64, 2048], P(None, None, ('slab', 'group')), may hold values from -10.1 to 0.1
Outputs:
- solution: float32 [64, 32768], P(None, ('slab', 'group'))
- coarse_error: float32 [64, 2048], P(None, ('slab', 'group'))
All inputs are finite; a program needn't handle non-finite values. No bound on the sum of `pattern` on one device may be relied on, other than what follows from the above.
Results may differ from a plain program's by a relative error of at most 0.0003.
Values sent between devices are 32-bit elements; how exact they have to be, the bound alone decides.
A program may use at most 64 MiB of HBM per device.

v0:
```python
import math

import jax
import jax.numpy as jnp
from jax import lax
from jax.sharding import PartitionSpec as P

SWEEPS = 2


damping = 0.8
smoothing = 0.67
highest = lax.Precision.HIGHEST


def extended(value, sides, width):
    for axis, dim in sides:
        devices, length = (lax.axis_size(axis), value.shape[dim])
        up = [(i, (i + 1) % devices) for i in range(devices - 1)]
        down = [(j, i) for i, j in up]
        last = lax.slice_in_dim(value, length - width, length, axis=dim)
        leading = lax.slice_in_dim(value, 0, width, axis=dim)
        before = lax.ppermute(last, axis, up)
        after = lax.ppermute(leading, axis, down)
        value = jnp.concatenate([before, value, after], axis=dim)
    return value


def prefix(part, axis, combine, identity):
    place = lax.axis_index(axis)
    gathered = jax.tree.map(lambda a: lax.all_gather(a, axis), part)
    state = jax.tree.map(lambda a, e: jnp.zeros_like(a) + jnp.asarray(e, a.dtype), part, identity)

    def one(turn, state):
        return combine(
            state, jax.tree.map(lambda a: lax.dynamic_index_in_dim(a, turn, 0, False), gathered)
        )

    return lax.fori_loop(0, place, one, state)


def fine_apply(iterate, blocks, pattern):
    padded = extended(iterate, ((("slab", "group"), 1),), 1)
    previous = padded[:, :-2] * pattern[0].astype(jnp.float32)[None, :]
    following = padded[:, 2:] * pattern[1].astype(jnp.float32)[None, :]
    product = jnp.einsum("abn,bn->an", blocks[0], previous, precision=highest)
    product = product + jnp.einsum("abn,bn->an", blocks[1], iterate, precision=highest)
    return product + jnp.einsum("abn,bn->an", blocks[2], following, precision=highest)


def block_apply(inverse, iterate):
    return jnp.einsum("abn,bn->an", inverse, iterate, precision=highest)


def selector_of(slot_map):
    block_width = slot_map.shape[1]
    return (slot_map[:, :, None] == jnp.arange(block_width, dtype=jnp.int32)[None, None, :]).astype(
        jnp.float32
    )


def restrict(residue, tentative, slot_map):
    num_modes = tentative.shape[0]
    num_blocks = slot_map.shape[0]
    block_width = slot_map.shape[1]
    weights = jnp.einsum("man,an->mn", tentative, residue, precision=highest) * (
        1.0 / math.sqrt(residue.shape[0])
    )
    weights = (
        weights.reshape(num_modes, num_blocks, block_width // num_modes)
        .transpose(1, 2, 0)
        .reshape(num_blocks, block_width)
    )
    return jnp.einsum("jqs,jq->sj", selector_of(slot_map), weights, precision=highest)


def extend(coarse, tentative, slot_map):
    num_modes = tentative.shape[0]
    num_blocks = slot_map.shape[0]
    block_width = slot_map.shape[1]
    weights = jnp.einsum("jqs,sj->jq", selector_of(slot_map), coarse, precision=highest)
    weights = (
        weights.reshape(num_blocks, block_width // num_modes, num_modes)
        .transpose(2, 0, 1)
        .reshape(num_modes, -1)
    )
    return jnp.einsum("man,mn->an", tentative, weights, precision=highest) * (
        1.0 / math.sqrt(tentative.shape[1])
    )


def coarse_sweep(coarse_rhs, coarse_inverse, coarse_lower, incoming):

    def coarse_advance(carried, items):
        rhs_block, inverse_block, lower_block = items
        solved = jnp.dot(
            inverse_block,
            rhs_block - jnp.dot(lower_block, carried, precision=highest),
            precision=highest,
        )
        return (solved, solved)

    unused, solved_all = lax.scan(
        coarse_advance,
        incoming,
        (coarse_rhs.T, jnp.moveaxis(coarse_inverse, 2, 0), jnp.moveaxis(coarse_lower, 2, 0)),
    )
    return solved_all.T


def combine(earlier, latter):
    matrix = jnp.einsum("ab...,bc...->ac...", latter[0], earlier[0], precision=highest)
    offset = jnp.einsum("ab...,b...->a...", latter[0], earlier[1], precision=highest) + latter[1]
    return (matrix, offset)


def block_maps(coarse_rhs, coarse_inverse, coarse_lower):
    matrices = -jnp.einsum("abj,bcj->acj", coarse_inverse, coarse_lower, precision=highest)
    offsets = jnp.einsum("abj,bj->aj", coarse_inverse, coarse_rhs, precision=highest)
    return (matrices, offsets)


def fold_maps(matrices, offsets):
    while matrices.shape[-1] > 1:
        matrices, offsets = combine(
            (matrices[..., 0::2], offsets[..., 0::2]), (matrices[..., 1::2], offsets[..., 1::2])
        )
    return (matrices[..., 0], offsets[..., 0])


def group_entry(matrices, offsets, start):

    def group_advance(carried, items):
        matrix, offset = items
        return (jnp.dot(matrix, carried, precision=highest) + offset, carried)

    unused, entries = lax.scan(group_advance, start, (jnp.moveaxis(matrices, 2, 0), offsets.T))
    return lax.dynamic_index_in_dim(entries, lax.axis_index("group"), 0, keepdims=False)


def body(
    right_side,
    fine_blocks,
    fine_inverse,
    pattern,
    tentative,
    slot_map,
    coarse_inverse,
    coarse_lower,
):
    solution = damping * block_apply(fine_inverse, right_side)
    solution = solution + damping * block_apply(
        fine_inverse, right_side - fine_apply(solution, fine_blocks, pattern)
    )
    residue = right_side - fine_apply(solution, fine_blocks, pattern)
    coarse_rhs = restrict(residue, tentative, slot_map)
    block_width = coarse_rhs.shape[0]
    own_count = coarse_rhs.shape[1]
    identity = (jnp.eye(block_width, dtype=jnp.float32), jnp.zeros((block_width,), jnp.float32))
    all_rhs, all_inverse, all_lower = (
        lax.all_gather(coarse_rhs, "group", axis=1, tiled=True),
        lax.all_gather(coarse_inverse, "group", axis=2, tiled=True),
        lax.all_gather(coarse_lower, "group", axis=2, tiled=True),
    )
    members = all_rhs.shape[1] // own_count
    matrices, offsets = block_maps(all_rhs, all_inverse, all_lower)
    matrices = matrices.reshape(block_width, block_width, members, own_count)
    offsets = offsets.reshape(block_width, members, own_count)
    member_mats, member_offs = fold_maps(matrices, offsets)
    group_mat, group_off = fold_maps(member_mats, member_offs)
    before_group = prefix((group_mat, group_off), "slab", combine, identity)
    incoming = group_entry(member_mats, member_offs, before_group[1])
    coarse_error = coarse_sweep(coarse_rhs, coarse_inverse, coarse_lower, incoming)
    correction = extend(coarse_error, tentative, slot_map)
    solution = (
        solution
        + correction
        - smoothing * block_apply(fine_inverse, fine_apply(correction, fine_blocks, pattern))
    )
    for sweep_index in range(SWEEPS):
        solution = solution + damping * block_apply(
            fine_inverse, right_side - fine_apply(solution, fine_blocks, pattern)
        )
    return (solution, coarse_error)


def solution(mesh):
    in_specs = (
        P(None, ("slab", "group")),
        P(None, None, None, ("slab", "group")),
        P(None, None, ("slab", "group")),
        P(None, ("slab", "group")),
        P(None, None, ("slab", "group")),
        P(("slab", "group"), None),
        P(None, None, ("slab", "group")),
        P(None, None, ("slab", "group")),
    )
    out_specs = (P(None, ("slab", "group")), P(None, ("slab", "group")))
    return jax.shard_map(body, mesh=mesh, in_specs=in_specs, out_specs=out_specs, check_vma=False)
```

profile of v0, /device:TPU:127, one launch (start us, length us, event | category | flops | bytes accessed | tf_op | source)
XLA Modules:
  0.0 282.0 jit_solution(7796157426249103355)
XLA Ops:
  7.2 2.1 copy_bitcast_fusion
  9.4 1.9 multiply_reduce_fusion.4
  11.4 4.9 %collective-permute-start = (f32[64,1]{1,0:T(8,128)S(1)}, f32[64,1]{1,0:T(8,128)S(1)}, u32[]{:S(2)}, u32[]{:S(2)}) collective-permute-start(f32[64,1]{1,0:T(8,128)S(1)} %get-tuple-element.215), channel_id=1, source_target_pairs={{0,1},{1,2},{2,3},{3,4},{4,5},{5,6},{6,7},{7,8},{8,9},{9,10},{10,1... | collective-permute-start | bytes 776 | tf_op jit(solution)/shard_map/ppermute | solution.py:23
  16.3 1.9 collective-permute-start.1
  18.3 8.8 %collective-permute-done.1 = f32[64,1]{1,0:T(8,128)S(1)} collective-permute-done((f32[64,1]{1,0:T(8,128)S(1)}, f32[64,1]{1,0:T(8,128)S(1)}, u32[]{:S(2)}, u32[]{:S(2)}) %collective-permute-start.1) | collective-permute-done | bytes 288 | tf_op jit(solution)/shard_map/ppermute | solution.py:24
  27.2 4.3 %fusion.26 = (f32[128,64]{0,1:T(8,128)S(1)}, f32[128,64]{0,1:T(8,128)S(1)}, f32[128,64]{0,1:T(8,128)S(1)}) fusion(f32[3,64,64,128]{3,2,1,0:T(8,128)} %param.15, f32[128,64]{0,1:T(8,128)S(1)} %get-tuple-element.217, f32[128,64]{0,1:T(8,128)S(1)} %get-tuple-element.213, f32[128,64]{0,1:T(8,128)S(1)} %get-tuple-element.212), kind=kLoop, calls=%fused_computation.40 | loop fusion | flops 3121152 | bytes 6488064 | tf_op jit(solution)/shard_map/abn,bn->an/dot_general | solution.py:47
  31.5 0.3 multiply_reduce_fusion.3
  32.0 1.9 collective-permute-start.2
  33.9 2.4 collective-permute-start.3
  36.3 0.7 dynamic-slice
  37.7 6.9 %collective-permute-done.3 = f32[64,1]{1,0:T(8,128)S(1)} collective-permute-done((f32[64,1]{1,0:T(8,128)S(1)}, f32[64,1]{1,0:T(8,128)S(1)}, u32[]{:S(2)}, u32[]{:S(2)}) %collective-permute-start.3) | collective-permute-done | bytes 288 | tf_op jit(solution)/shard_map/ppermute | solution.py:24
  44.7 4.1 %fusion.27 = (f32[128,64]{0,1:T(8,128)S(1)}, f32[128,64]{0,1:T(8,128)S(1)}, f32[128,64]{0,1:T(8,128)S(1)}) fusion(f32[3,64,64,128]{3,2,1,0:T(8,128)} %param.15, f32[128,64]{0,1:T(8,128)S(1)} %bitcast.392, f32[128,64]{0,1:T(8,128)S(1)} %get-tuple-element.209, f32[128,64]{0,1:T(8,128)S(1)} %get-tuple-element.208), kind=kLoop, calls=%fused_computation.41 | loop fusion | flops 3121152 | bytes 6488064 | tf_op jit(solution)/shard_map/abn,bn->an/dot_general | solution.py:47
  49.0 0.3 fusion.49
  49.4 10.1 %all_gather.18 = f32[64,64]{0,1:T(8,128)S(1)} all-gather(f32[64,8]{0,1:T(8,128)S(1)} %bitcast.410), channel_id=1, replica_groups=mesh['slab'=32,'group'=8] {'group'}, dimensions={1}, use_global_device_ids=true | all-gather | bytes 18432 | tf_op jit(solution)/shard_map/all_gather | solution.py:161
  59.4 5.0 %fusion.93 = f32[64,1,64]{2,1,0:T(1,128)S(1)} fusion(f32[64,64,1]{0,2,1:T(1,128)S(1)} %bitcast.395, f32[64,64,64]{1,0,2:T(8,128)} %all-gather.7.cloned.1.call-done), kind=kOutput, calls=%fused_computation.159 | convolution fusion | flops 3145728 | bytes 1081344 | tf_op jit(solution)/shard_map/abj,bj->aj/dot_general | solution.py:119
  64.5 3.9 %all-gather.5.cloned.1.call-done = f32[64,64,64]{1,0,2:T(8,128)} async-done(((f32[64,64,8]{1,0,2:T(8,128)}), f32[64,64,64]{1,0,2:T(8,128)}) %all-gather.5.cloned.1.call-update) | async-done | bytes 1048592 | tf_op jit(solution)/shard_map/all_gather | solution.py:163
  68.4 5.8 %convolution_negate_fusion = f32[64,64,64]{2,1,0:T(8,128)S(1)} fusion(f32[64,64,64]{1,0,2:T(8,128)} %all-gather.5.cloned.1.call-done, f32[64,64,64]{1,0,2:T(8,128)} %all-gather.7.cloned.1.call-done), kind=kOutput, calls=%fused_computation.60 | convolution fusion | flops 201588736 | bytes 3145728 | tf_op jit(solution)/shard_map/abj,bcj->acj/dot_general | solution.py:118
  74.1 1.2 convolution_bitcast_fusion.3
  75.4 1.0 fusion.41
  76.4 0.6 convolution_bitcast_fusion.4
  77.0 0.5 fusion.44
  77.6 0.4 fusion.47
  78.0 0.3 fusion.36
  78.3 0.3 convolution_bitcast_fusion.5
  79.6 0.2 dynamic-update-slice
  79.8 57.0 %all-reduce = f32[2048]{0:T(1024)S(1)} all-reduce(f32[2048]{0:T(1024)S(1)} %dynamic-update-slice), channel_id=3, replica_groups=mesh['slab'=32,'group'=8] {'slab'}, use_global_device_ids=true, to_apply=%add | all-reduce | flops 2048 | bytes 16384
  136.9 37.1 %all-gather = f32[2048,64,1]{1,2,0:T(1,128)S(1)} all-gather(f32[64,64,1]{1,2,0:T(1,128)S(1)} %copy.53), channel_id=2, replica_groups=mesh['slab'=32,'group'=8] {'slab'}, dimensions={0}, use_global_device_ids=true | all-gather | bytes 540672 | tf_op jit(solution)/shard_map/all_gather | solution.py:31
  174.0 2.9 %while.36 = (s32[]{:T(128)}, f32[64]{0:T(128)S(1)}, s32[]{:T(128)}, f32[32,64,64]{2,1,0:T(8,128)S(1)}, f32[32,64]{1,0:T(8,128)S(1)}, /*index=5*/s32[]{:T(128)}, s32[]{:T(128)}, s32[]{:T(128)}) while((s32[]{:T(128)}, f32[64]{0:T(128)S(1)}, s32[]{:T(128)}, f32[32,64,64]{2,1,0:T(8,128)S(1)}, f32[32,64]{1,0:T(8,128)S(1)}, /*index=5*/s32[]{:T(128)}, ...), condition=%wide.region_1.2_spmd, body=%wide.region_0.1_spmd.sunk | while | flops 49221 | bytes 35703 | solution.py:39
  176.9 1.5 while.37
  178.5 15.2 %while.38 = (s32[]{:T(128)}, f32[64]{0:T(128)S(1)}, f32[8,64]{1,0:T(8,128)S(1)}, f32[8,64,64]{2,1,0:T(8,128)}, f32[8,64]{1,0:T(8,128)S(1)}, /*index=5*/f32[8,64,64]{2,1,0:T(8,128)}, s32[]{:T(128)}, s32[]{:T(128)}) while((s32[]{:T(128)}, f32[64]{0:T(128)S(1)}, f32[8,64]{1,0:T(8,128)S(1)}, f32[8,64,64]{2,1,0:T(8,128)}, f32[8,64]{1,0:T(8,128)S(1)}, ...), condition=%wide.region_5.6_spmd, body=%wide.region_4.5_spmd.sunk | while | flops 98370 | bytes 68953 | solution.py:103
  178.5 0.9 fusion.127
  179.4 0.9 fusion.128
  180.4 0.9 fusion.127
  181.3 0.9 fusion.128
  182.3 0.9 fusion.127
  183.2 0.9 fusion.128
  184.2 0.9 fusion.127
  185.1 0.9 fusion.128
  186.1 0.9 fusion.127
  187.0 0.9 fusion.128
  188.0 0.9 fusion.127
  188.9 0.9 fusion.128
  189.9 0.9 fusion.127
  190.8 0.9 fusion.128
  191.8 0.9 fusion.127
  192.7 0.9 fusion.128
  193.7 0.4 fusion.48
  194.3 0.9 multiply_reduce_fusion.5
  195.4 31.6 %collective-permute-start.4 = (f32[64,1]{1,0:T(8,128)S(1)}, f32[64,1]{1,0:T(8,128)S(1)}, u32[]{:S(2)}, u32[]{:S(2)}) collective-permute-start(f32[64,1]{1,0:T(8,128)S(1)} %get-tuple-element.205), channel_id=1, source_target_pairs={{0,1},{1,2},{2,3},{3,4},{4,5},{5,6},{6,7},{7,8},{8,9},{9,10},{10,1... | collective-permute-start | bytes 776 | tf_op jit(solution)/shard_map/ppermute | solution.py:23
  227.0 1.9 collective-permute-start.5
  228.9 8.7 %collective-permute-done.5 = f32[64,1]{1,0:T(8,128)S(1)} collective-permute-done((f32[64,1]{1,0:T(8,128)S(1)}, f32[64,1]{1,0:T(8,128)S(1)}, u32[]{:S(2)}, u32[]{:S(2)}) %collective-permute-start.5) | collective-permute-done | bytes 288 | tf_op jit(solution)/shard_map/ppermute | solution.py:24
  237.8 4.0 %fusion.28 = (f32[128,64]{0,1:T(8,128)S(1)}, f32[128,64]{0,1:T(8,128)S(1)}, f32[128,64]{0,1:T(8,128)S(1)}) fusion(f32[3,64,64,128]{3,2,1,0:T(8,128)} %param.15, f32[128,64]{0,1:T(8,128)S(1)} %get-tuple-element.207, f32[128,64]{0,1:T(8,128)S(1)} %get-tuple-element.203, f32[128,64]{0,1:T(8,128)S(1)} %get-tuple-element.202), kind=kLoop, calls=%fused_computation.42 | loop fusion | flops 3121152 | bytes 6488064
  242.2 0.3 multiply_reduce_fusion.2
  242.6 2.2 collective-permute-start.6
  244.8 2.4 collective-permute-start.7
  247.2 8.2 %collective-permute-done.7 = f32[64,1]{1,0:T(8,128)S(1)} collective-permute-done((f32[64,1]{1,0:T(8,128)S(1)}, f32[64,1]{1,0:T(8,128)S(1)}, u32[]{:S(2)}, u32[]{:S(2)}) %collective-permute-start.7) | collective-permute-done | bytes 288 | tf_op jit(solution)/shard_map/ppermute | solution.py:24
  255.6 4.2 %fusion.29 = (f32[128,64]{0,1:T(8,128)S(1)}, f32[128,64]{0,1:T(8,128)S(1)}, f32[128,64]{0,1:T(8,128)S(1)}) fusion(f32[3,64,64,128]{3,2,1,0:T(8,128)} %param.15, f32[128,64]{0,1:T(8,128)S(1)} %bitcast.393, f32[128,64]{0,1:T(8,128)S(1)} %get-tuple-element.199, f32[128,64]{0,1:T(8,128)S(1)} %get-tuple-element.198), kind=kLoop, calls=%fused_computation.43 | loop fusion | flops 3121152 | bytes 6488064 | tf_op jit(solution)/shard_map/abn,bn->an/dot_general | solution.py:47
  259.8 0.3 multiply_reduce_fusion.1
  260.2 1.9 collective-permute-start.8
  262.1 2.4 collective-permute-start.9
  264.6 8.2 %collective-permute-done.9 = f32[64,1]{1,0:T(8,128)S(1)} collective-permute-done((f32[64,1]{1,0:T(8,128)S(1)}, f32[64,1]{1,0:T(8,128)S(1)}, u32[]{:S(2)}, u32[]{:S(2)}) %collective-permute-start.9) | collective-permute-done | bytes 288 | tf_op jit(solution)/shard_map/ppermute | solution.py:24
  272.9 1.2 fusion.30
  274.2 0.3 multiply_reduce_fusion
  274.5 0.6 bitcast_add_fusion
  (148 shorter events, 7.7 us)
Async XLA Ops:
  7.2 11.1 %copy-start.4 = (s32[2,128]{1,0:T(2,128)S(1)}, s32[2,128]{1,0:T(2,128)}, u32[]{:S(2)}) copy-start(s32[2,128]{1,0:T(2,128)} %param.17) | copy-start | bytes 3076
  7.2 52.3 %all-gather.7.cloned.1.call-start = ((), (), s32[]{:S(2)}) async-start(), calls=%async_computation.1 | async-start | bytes 2359296 | tf_op jit(solution)/shard_map/all_gather | solution.py:162
  9.3 59.1 %all-gather.5.cloned.1.call-start = ((), (), s32[]{:S(2)}) async-start(), calls=%async_computation | async-start | bytes 2359296 | tf_op jit(solution)/shard_map/all_gather | solution.py:163
  11.4 6.9 %collective-permute-start = (f32[64,1]{1,0:T(8,128)S(1)}, f32[64,1]{1,0:T(8,128)S(1)}, u32[]{:S(2)}, u32[]{:S(2)}) collective-permute-start(f32[64,1]{1,0:T(8,128)S(1)} %get-tuple-element.215), channel_id=1, source_target_pairs={{0,1},{1,2},{2,3},{3,4},{4,5},{5,6},{6,7},{7,8},{8,9},{9,10},{10,1... | collective-permute-start | bytes 776 | tf_op jit(solution)/shard_map/ppermute | solution.py:23
  16.3 10.8 %collective-permute-start.1 = (f32[64,1]{1,0:T(8,128)S(1)}, f32[64,1]{1,0:T(8,128)S(1)}, u32[]{:S(2)}, u32[]{:S(2)}) collective-permute-start(f32[64,1]{1,0:T(8,128)S(1)} %get-tuple-element.214), channel_id=1, source_target_pairs={{1,0},{2,1},{3,2},{4,3},{5,4},{6,5},{7,6},{8,7},{9,8},{10,9},{11,1... | collective-permute-start | bytes 776 | tf_op jit(solution)/shard_map/ppermute | solution.py:24
  27.1 4.3 %copy-start.1 = (f32[64,128]{1,0:T(8,128)S(1)}, f32[64,128]{1,0:T(8,128)}, u32[]{:S(2)}) copy-start(f32[64,128]{1,0:T(8,128)} %param.14) | copy-start | bytes 98308
  27.2 4.4 %copy-start = (f32[64,64,128]{2,1,0:T(8,128)S(1)}, f32[64,64,128]{2,1,0:T(8,128)}, u32[]{:S(2)}) copy-start(f32[64,64,128]{2,1,0:T(8,128)} %param.16) | copy-start | bytes 6291460
  31.5 4.8 %copy-start.6 = (u32[256]{0:T(256)S(1)}, u32[256]{0:T(256)}, u32[]{:S(2)}) copy-start(u32[256]{0:T(256)} %constant.71) | copy-start | bytes 3076
  32.0 5.7 %collective-permute-start.2 = (f32[64,1]{1,0:T(8,128)S(1)}, f32[64,1]{1,0:T(8,128)S(1)}, u32[]{:S(2)}, u32[]{:S(2)}) collective-permute-start(f32[64,1]{1,0:T(8,128)S(1)} %get-tuple-element.211), channel_id=1, source_target_pairs={{0,1},{1,2},{2,3},{3,4},{4,5},{5,6},{6,7},{7,8},{8,9},{9,10},{10,1... | collective-permute-start | bytes 776 | tf_op jit(solution)/shard_map/ppermute | solution.py:23
  33.9 10.7 %collective-permute-start.3 = (f32[64,1]{1,0:T(8,128)S(1)}, f32[64,1]{1,0:T(8,128)S(1)}, u32[]{:S(2)}, u32[]{:S(2)}) collective-permute-start(f32[64,1]{1,0:T(8,128)S(1)} %get-tuple-element.210), channel_id=1, source_target_pairs={{1,0},{2,1},{3,2},{4,3},{5,4},{6,5},{7,6},{8,7},{9,8},{10,9},{11,1... | collective-permute-start | bytes 776 | tf_op jit(solution)/shard_map/ppermute | solution.py:24
  44.6 4.1 %copy-start.2 = (f32[4,64,128]{2,1,0:T(8,128)S(1)}, f32[4,64,128]{2,1,0:T(8,128)}, u32[]{:S(2)}) copy-start(f32[4,64,128]{2,1,0:T(8,128)} %param.18) | copy-start | bytes 393220
  44.7 4.4 %copy-start.5 = (s32[8,64]{1,0:T(8,128)S(1)}, s32[8,64]{1,0:T(8,128)}, u32[]{:S(2)}) copy-start(s32[8,64]{1,0:T(8,128)} %param.19) | copy-start | bytes 6148
  193.7 48.1 %copy-start.3 = (f32[8,64]{1,0:T(8,128)}, f32[8,64]{1,0:T(8,128)S(1)}, u32[]{:S(2)}) copy-start(f32[8,64]{1,0:T(8,128)S(1)} %get-tuple-element.107) | copy-start | bytes 6148
  195.4 33.6 %collective-permute-start.4 = (f32[64,1]{1,0:T(8,128)S(1)}, f32[64,1]{1,0:T(8,128)S(1)}, u32[]{:S(2)}, u32[]{:S(2)}) collective-permute-start(f32[64,1]{1,0:T(8,128)S(1)} %get-tuple-element.205), channel_id=1, source_target_pairs={{0,1},{1,2},{2,3},{3,4},{4,5},{5,6},{6,7},{7,8},{8,9},{9,10},{10,1... | collective-permute-start | bytes 776 | tf_op jit(solution)/shard_map/ppermute | solution.py:23
  227.0 10.7 %collective-permute-start.5 = (f32[64,1]{1,0:T(8,128)S(1)}, f32[64,1]{1,0:T(8,128)S(1)}, u32[]{:S(2)}, u32[]{:S(2)}) collective-permute-start(f32[64,1]{1,0:T(8,128)S(1)} %get-tuple-element.204), channel_id=1, source_target_pairs={{1,0},{2,1},{3,2},{4,3},{5,4},{6,5},{7,6},{8,7},{9,8},{10,9},{11,1... | collective-permute-start | bytes 776 | tf_op jit(solution)/shard_map/ppermute | solution.py:24
  242.2 30.7 %slice-start = ((s8[6291456]{0:T(1024)(128)(4,1)}), s8[4194304]{0:T(1024)(128)(4,1)S(1)}, s32[]{:S(2)}) async-start(s8[6291456]{0:T(1024)(128)(4,1)} %bitcast.383), calls=%async_computation.2 | async-start | bytes 8388608
  242.6 4.6 %collective-permute-start.6 = (f32[64,1]{1,0:T(8,128)S(1)}, f32[64,1]{1,0:T(8,128)S(1)}, u32[]{:S(2)}, u32[]{:S(2)}) collective-permute-start(f32[64,1]{1,0:T(8,128)S(1)} %get-tuple-element.201), channel_id=1, source_target_pairs={{0,1},{1,2},{2,3},{3,4},{4,5},{5,6},{6,7},{7,8},{8,9},{9,10},{10,1... | collective-permute-start | bytes 776 | tf_op jit(solution)/shard_map/ppermute | solution.py:23
  244.8 10.7 %collective-permute-start.7 = (f32[64,1]{1,0:T(8,128)S(1)}, f32[64,1]{1,0:T(8,128)S(1)}, u32[]{:S(2)}, u32[]{:S(2)}) collective-permute-start(f32[64,1]{1,0:T(8,128)S(1)} %get-tuple-element.200), channel_id=1, source_target_pairs={{1,0},{2,1},{3,2},{4,3},{5,4},{6,5},{7,6},{8,7},{9,8},{10,9},{11,1... | collective-permute-start | bytes 776 | tf_op jit(solution)/shard_map/ppermute | solution.py:24
  255.6 17.3 %slice-start.1 = ((s8[6291456]{0:T(1024)(128)(4,1)}), s8[2097152]{0:T(1024)(128)(4,1)S(1)}, s32[]{:S(2)}) async-start(s8[6291456]{0:T(1024)(128)(4,1)} %bitcast.383), calls=%async_computation.3 | async-start | bytes 4194304
  260.2 4.3 %collective-permute-start.8 = (f32[64,1]{1,0:T(8,128)S(1)}, f32[64,1]{1,0:T(8,128)S(1)}, u32[]{:S(2)}, u32[]{:S(2)}) collective-permute-start(f32[64,1]{1,0:T(8,128)S(1)} %get-tuple-element.197), channel_id=1, source_target_pairs={{0,1},{1,2},{2,3},{3,4},{4,5},{5,6},{6,7},{7,8},{8,9},{9,10},{10,1... | collective-permute-start | bytes 776 | tf_op jit(solution)/shard_map/ppermute | solution.py:23
  262.1 10.7 %collective-permute-start.9 = (f32[64,1]{1,0:T(8,128)S(1)}, f32[64,1]{1,0:T(8,128)S(1)}, u32[]{:S(2)}, u32[]{:S(2)}) collective-permute-start(f32[64,1]{1,0:T(8,128)S(1)} %get-tuple-element.196), channel_id=1, source_target_pairs={{1,0},{2,1},{3,2},{4,3},{5,4},{6,5},{7,6},{8,7},{9,8},{10,9},{11,1... | collective-permute-start | bytes 776 | tf_op jit(solution)/shard_map/ppermute | solution.py:24
Sparse Core Ops, SparseCore 0:
  9.9 28.7 all-gather.6
  40.5 27.8 all-gather.4
where the time goes:
time: 284 us; the launch traced here: 282 us
  blocking collectives  104 us (37%)
  starting transfers between devices  53.7 us (19%)
  waiting for transfers between devices  44.8 us (16%)
  matrix products  35.2 us (12%)
  other arithmetic  23.2 us (8%)
  between operations  15.4 us (5%)
  local copies, waits for them, and re-layouts  5.24 us (2%)
    unnamed x1, blocking collectives  57 us
    ppermute x5, starting transfers between devices, extended(): before = lax.ppermute(last, axis, up)  42.5 us
    ppermute x5, waiting for transfers between devices, extended(): after = lax.ppermute(leading, axis, down)  40.8 us
    all_gather x1, blocking collectives, prefix(): gathered = jax.tree.map(lambda a: lax.all_gather(a, axis), part)  37.1 us
    dot_general x4, other arithmetic, fine_apply(): jnp.einsum('abn,bn->an', blocks[1], iterate, precision=highest)  13.8 us
    ppermute x5, starting transfers between devices, extended(): after = lax.ppermute(leading, axis, down)  11.1 us
    all_gather x1, blocking collectives, body(): lax.all_gather(coarse_rhs, 'group', axis=1, tiled=True)  10.1 us
    dot_general x8, matrix products, coarse_advance(): jnp.dot(inverse_block, rhs_block - jnp.dot(lower_block, carried, precisio...  7.44 us
  transfers between devices with their start and end apart: 12, of which 6 were waited for; matrix products, arithmetic and copies ran while one was open for 6% of the time, Pallas kernels for 0%

commit v1 on v0

v1 whole, which is shorter than its diff:
```python
import functools
import math

import jax
import jax.numpy as jnp
from jax import lax
from jax.experimental import pallas as pl
from jax.experimental.pallas import tpu as pltpu
from jax.sharding import PartitionSpec as P

DAMP = 0.8
SMOOTH = 0.67
F32 = jnp.float32
BF16 = jnp.bfloat16
MESH = pl.DeviceIdType.MESH

NN = (((1,), (0,)), ((), ()))
NT = (((1,), (1,)), ((), ()))


def split(x):
    hi = x.astype(BF16)
    return hi, (x - hi.astype(F32)).astype(BF16)


def dot1(a, b, dims=NN):
    return lax.dot_general(a, b, dims, preferred_element_type=F32)


def dot3(a, b, dims=NN):
    ah, al = split(a)
    bh, bl = split(b)
    return dot1(ah, bh, dims) + (dot1(ah, bl, dims) + dot1(al, bh, dims))


def dot2(a, b, dims=NN):
    ah, al = split(a)
    return dot1(ah, b, dims) + dot1(al, b, dims)


def iota(shape, dim):
    return lax.broadcasted_iota(jnp.int32, shape, dim)


def fold_rows(parts):
    row = iota((8, 128), 0)

    def mix(a, b, mask, shift):
        return jnp.where(mask, a, b) + pltpu.roll(jnp.where(mask, b, a), shift, 0)

    q = [parts[(i + 3) % 8] for i in range(8)]
    y = [mix(q[k], q[k + 4], ((row - k) & 7) < 4, 4) for k in range(4)]
    z = [mix(y[k], y[k + 2], ((row - k) & 3) >= 2, 2) for k in range(2)]
    return mix(z[0], z[1], (row & 1) == 1, 1)


def row_sum(x):
    x = x + pltpu.roll(x, 4, 0)
    x = x + pltpu.roll(x, 2, 0)
    return x + pltpu.roll(x, 1, 0)


def matvec(terms, width, emit):
    def one(g, unused):
        parts = []
        for a in range(8):
            total = None
            for load, v in terms:
                product = load(g * 8 + a) * v
                total = product if total is None else total + product
            parts.append(jnp.sum(total.reshape(width // 8, 8, 128), axis=0))
        emit(pl.ds(pl.multiple_of(g * 8, 8), 8), fold_rows(parts))
        return unused

    lax.fori_loop(0, width // 8, one, 0)


def pack_matrix(m):
    return jnp.concatenate([m[:32, :], m[32:, :]], axis=1)


def unpack_matrix(p):
    return jnp.concatenate([p[:, :64], p[:, 64:]], axis=0)


def scan_products(ref, count):
    half = 1
    while half < count:
        for start in range(0, count, 2 * half):
            mid = start + half
            left = pl.ds(start * 64, half * 64)
            ref[left, :] = dot3(ref[left, :], ref[pl.ds(mid * 64, 64), :])
        half *= 2


def scan_prefix(ref, count):
    half = 1
    while half < count:
        for start in range(0, count, 2 * half):
            mid = start + half
            right = pl.ds(mid * 64, half * 64)
            ref[right, :] = dot3(ref[right, :], ref[pl.ds((mid - 1) * 64, 64), :])
        half *= 2


def diagonal(x, count):
    return jnp.where(iota(x.shape, 0) == iota(x.shape, 1) // 64, x, 0.0)


def lanes_folded(x):
    t = x[:, 0:128] + x[:, 128:256] + x[:, 256:384] + x[:, 384:512]
    return t[:, :64] + t[:, 64:]


def padded(x):
    return jnp.concatenate([x, jnp.zeros_like(x)], axis=1)


def kernel(
    nz, nx, ng,
    b_h, f_h, i_h, pat_h, tent_h, slot_h, ci_h, cl_h,
    sol_ref, ce_ref,
    F, I, b, pat, tent, slot, ci, cl,
    work, res, corr,
    cis, Zl, Pl, Z1, Zm1, Z2, Zm2, Zm3,
    Xl, W1, W2, W3,
    RM1, RM2, RM3, RV1, RV2, RV3, halo_out, halo_in,
    load_sem, m_send, m_recv, v_send, v_recv, h_send, h_recv,
):
    slab, g = lax.axis_index("slab"), lax.axis_index("group")
    z, x = slab // nx, slab % nx
    ns = nz * nx

    copies = []
    for k, (src, dst) in enumerate(
        [(ci_h, ci), (cl_h, cl), (i_h, I), (b_h, b), (slot_h, slot), (pat_h, pat),
         (f_h.at[1], F.at[1]), (f_h.at[0], F.at[0]), (f_h.at[2], F.at[2]), (tent_h, tent)]
    ):
        copy = pltpu.make_async_copy(src, dst, load_sem.at[k])
        copy.start()
        copies.append(copy)
    ci_c, cl_c, i_c, b_c, slot_c, pat_c, f1_c, f0_c, f2_c, tent_c = copies

    def in_group(o):
        return (slab, lax.rem(g + o, ng))

    def along_x(o):
        return (z * nx + lax.rem(x + o, nx), g)

    def along_z(o):
        return (lax.rem(z + o, nz) * nx + x, g)

    at_end, at_start = g == ng - 1, g == 0
    right = (jnp.where(at_end, lax.rem(slab + 1, ns), slab), lax.rem(g + 1, ng))
    left = (jnp.where(at_start, lax.rem(slab + ns - 1, ns), slab), lax.rem(g + ng - 1, ng))

    barrier = pltpu.get_barrier_semaphore()
    peers = [in_group(o) for o in range(1, ng)] + [along_x(o) for o in range(1, nx)]
    peers += [along_z(o) for o in range(1, nz)] + [right, left]
    for peer in peers:
        pl.semaphore_signal(barrier, inc=1, device_id=peer, device_id_type=MESH)

    row64, lane64 = iota((64, 64), 0), iota((64, 64), 1)
    eye = (row64 == lane64).astype(F32)
    ci_c.wait()
    cl_c.wait()
    for j in range(8):
        cij = ci[:, j, :]
        cis[pl.ds(j * 64, 64), :] = cij
        m = -dot3(cij, cl[:, j, :])
        Pl[pl.ds(j * 64, 64), :] = m
        e = m.T
        Zl[pl.ds(j * 64, 64), :] = e
        Xl[pl.ds(j * 64, 64), :] = e
    scan_products(Zl, 8)

    pl.semaphore_wait(barrier, len(peers))

    def gather_start(ref, own, target, count, send, recv):
        started = []
        for o in range(1, count):
            copy = pltpu.make_async_remote_copy(
                src_ref=ref.at[own],
                dst_ref=ref.at[own],
                send_sem=send.at[o],
                recv_sem=recv.at[own],
                device_id=target(o),
                device_id_type=MESH,
            )
            copy.start()
            started.append(copy)
        return started

    def gather_wait(started, ref, own, count, recv):
        for o in range(1, count):
            other = lax.rem(own + o, count)
            pltpu.make_async_copy(ref.at[other], ref.at[other], recv.at[other]).wait()
        for copy in started:
            copy.wait_send()

    RM1[g] = pack_matrix(Zl[0:64, :])
    rm1 = gather_start(RM1, g, in_group, ng, m_send.at[0], m_recv.at[0])

    lane8, lane = iota((8, 128), 1), iota((64, 128), 1)
    has_left = jnp.logical_not(jnp.logical_and(slab == 0, at_start))
    has_right = jnp.logical_not(jnp.logical_and(slab == ns - 1, at_end))

    def halo_start(turn, ref):
        to_right, to_left = jnp.zeros((8, 128), F32), jnp.zeros((8, 128), F32)
        for k in range(8):
            piece = ref[pl.ds(8 * k, 8), :]
            to_right = jnp.where(lane8 == k, pltpu.roll(piece, k + 1, 1), to_right)
            to_left = jnp.where(lane8 == k, pltpu.roll(piece, k, 1) if k else piece, to_left)
        halo_out[turn, 0] = to_right
        halo_out[turn, 1] = to_left
        started = []
        for side, peer in ((0, right), (1, left)):
            copy = pltpu.make_async_remote_copy(
                src_ref=halo_out.at[turn, side],
                dst_ref=halo_in.at[turn, side],
                send_sem=h_send.at[turn, side],
                recv_sem=h_recv.at[turn, side],
                device_id=peer,
                device_id_type=MESH,
            )
            copy.start()
            started.append(copy)
        return started

    def fine_apply(turn, ref, started, emit):
        for copy in started:
            copy.wait()
        from_left = jnp.where(has_left, halo_in[turn, 0], 0.0)
        from_right = jnp.where(has_right, halo_in[turn, 1], 0.0)
        value = ref[...]
        before, after = [], []
        for k in range(8):
            piece = value[8 * k : 8 * k + 8]
            edge = pltpu.roll(from_left, (128 - k) % 128, 1) if k else from_left
            before.append(jnp.where(lane8 == 0, edge, pltpu.roll(piece, 1, 1)))
            edge = pltpu.roll(from_right, 127 - k, 1)
            after.append(jnp.where(lane8 == 127, edge, pltpu.roll(piece, 127, 1)))
        previous = jnp.concatenate(before, axis=0) * pat[0:1, :].astype(F32)
        following = jnp.concatenate(after, axis=0) * pat[1:2, :].astype(F32)
        matvec(
            [
                (lambda a: F[1, a], value),
                (lambda a: F[0, a], previous),
                (lambda a: F[2, a], following),
            ],
            64,
            emit,
        )

    def block_apply(value, emit):
        matvec([(lambda a: I[a], value)], 64, emit)

    def to_residue(rows, y):
        res[rows, :] = b[rows, :] - y

    def sweep(turn, ref, started):
        fine_apply(turn, ref, started, to_residue)

        def emit(rows, y):
            ref[rows, :] = ref[rows, :] + DAMP * y

        block_apply(res[...], emit)

    def first(rows, y):
        work[rows, :] = DAMP * y

    i_c.wait()
    b_c.wait()
    block_apply(b[...], first)
    h0 = halo_start(0, work)

    slot_c.wait()
    q, col = iota((64, 512), 0), iota((64, 512), 1)
    pick = (q == (col % 16) * 4 + col // 128).astype(BF16)
    own_block = iota((8, 512), 0) == (iota((8, 512), 1) % 128) // 16
    slots = dot1(slot[...].astype(F32).astype(BF16), pick)
    slots = row_sum(jnp.where(own_block, slots, 0.0))
    slots = jnp.concatenate([slots] * 8, axis=0)
    GT = (slots == q.astype(F32)).astype(BF16)

    pat_c.wait()
    f0_c.wait()
    f1_c.wait()
    f2_c.wait()
    sweep(0, work, h0)
    h1 = halo_start(1, work)

    def upward(started, ref, own, count, recv, full, masked):
        gather_wait(started, ref, own, count, recv)
        for k in range(count):
            e = unpack_matrix(ref[k])
            rows = pl.ds(k * 64, 64)
            if full is not None:
                full[rows, :] = e
            masked[rows, :] = jnp.where(k < own, e, eye)
        if full is not None:
            scan_products(full, count)
        scan_products(masked, count)

    def later(ref, h, count):
        return ref[pl.ds((h + 1) * 64, 64), :] if h + 1 < count else eye

    upward(rm1, RM1, g, ng, m_recv.at[0], Z1, Zm1)
    RM2[x] = pack_matrix(Z1[0:64, :])
    rm2 = gather_start(RM2, x, along_x, nx, m_send.at[1], m_recv.at[1])
    for h in range(ng):
        W1[pl.ds(h * 64, 64), :] = jnp.concatenate(
            [later(Z1, h, ng), jnp.where(h < g, later(Zm1, h, ng), 0.0)], axis=1
        )

    fine_apply(1, work, h1, to_residue)
    tent_c.wait()
    residue = res[...]
    values = []
    for m in range(4):
        weight = jnp.sum((tent[m] * residue).reshape(8, 8, 128), axis=0)
        values.append(row_sum(weight) * (1.0 / math.sqrt(64)))
    spread = jnp.where(own_block, jnp.concatenate(values, axis=1), 0.0)
    rhs = dot2(spread, GT, NT)
    offsets = diagonal(dot3(rhs, cis[...], NT), 8)
    after_own = jnp.concatenate([Zl[64:512, :], eye], axis=0)
    RV1[g] = padded(row_sum(dot3(offsets, after_own)))
    rv1 = gather_start(RV1, g, in_group, ng, v_send.at[0], v_recv.at[0])

    upward(rm2, RM2, x, nx, m_recv.at[1], Z2, Zm2)
    RM3[z] = pack_matrix(Z2[0:64, :])
    rm3 = gather_start(RM3, z, along_z, nz, m_send.at[2], m_recv.at[2])
    for h in range(nx):
        W2[pl.ds(h * 64, 64), :] = jnp.concatenate(
            [later(Z2, h, nx), jnp.where(h < x, later(Zm2, h, nx), 0.0)], axis=1
        )

    own = lanes_folded(offsets)
    row8 = iota((8, 64), 0)
    carried = jnp.broadcast_to(own[0:1], (8, 64))
    local = carried
    for j in range(1, 8):
        carried = dot3(carried, Xl[pl.ds(j * 64, 64), :]) + own[j : j + 1]
        local = jnp.where(row8 >= j, carried, local)
    scan_prefix(Pl, 8)

    def inflow(ref, weights, count):
        total = None
        for h in range(count):
            term = dot3(ref[h][:, :64], weights[pl.ds(h * 64, 64), :])
            total = term if total is None else total + term
        return total

    gather_wait(rv1, RV1, g, ng, v_recv.at[0])
    flow1 = inflow(RV1, W1, ng)
    RV2[x] = padded(flow1[:, :64])
    rv2 = gather_start(RV2, x, along_x, nx, v_send.at[1], v_recv.at[1])

    upward(rm3, RM3, z, nz, m_recv.at[2], None, Zm3)
    A1 = Zm1[0:64, :]
    A21 = dot3(Zm2[0:64, :], A1)
    for h in range(nz):
        W3[pl.ds(h * 64, 64), :] = jnp.where(h < z, later(Zm3, h, nz), 0.0)
    W3[...] = dot3(W3[...], A21)

    gather_wait(rv2, RV2, x, nx, v_recv.at[1])
    flow2 = inflow(RV2, W2, nx)
    RV3[z] = padded(flow2[:, :64])
    rv3 = gather_start(RV3, z, along_z, nz, v_send.at[2], v_recv.at[2])
    nearer = dot3(flow2[:, 64:], A1) + flow1[:, 64:]
    gather_wait(rv3, RV3, z, nz, v_recv.at[2])
    incoming = inflow(RV3, W3, nz) + nearer

    coarse = local + lanes_folded(diagonal(dot3(incoming, Pl[...], NT), 8))
    ce_ref[...] = coarse
    weights = jnp.where(own_block, dot2(coarse, GT), 0.0)
    total = None
    for m in range(4):
        w = row_sum(weights[:, m * 128 : m * 128 + 128]) * (1.0 / math.sqrt(64))
        term = tent[m] * jnp.concatenate([w] * 8, axis=0)
        total = term if total is None else total + term
    corr[...] = total
    h2 = halo_start(2, corr)

    def to_res(rows, y):
        res[rows, :] = y

    fine_apply(2, corr, h2, to_res)

    def prolong(rows, y):
        work[rows, :] = work[rows, :] + corr[rows, :] - SMOOTH * y

    block_apply(res[...], prolong)
    h3 = halo_start(3, work)
    sweep(3, work, h3)
    h4 = halo_start(4, work)
    sweep(4, work, h4)
    sol_ref[...] = work[...]


def body(nz, nx, ng, right_side, fine_blocks, fine_inverse, pattern, tentative, slot_map, coarse_inverse, coarse_lower):
    vmem = lambda *shape: pltpu.VMEM(shape, F32)
    dma = lambda *shape: pltpu.SemaphoreType.DMA(shape)
    top = max(nz, nx, ng)
    scratch = [
        vmem(3, 64, 64, 128), vmem(64, 64, 128), vmem(64, 128), pltpu.VMEM((2, 128), jnp.int32), vmem(4, 64, 128),
        pltpu.VMEM((8, 64), jnp.int32), vmem(64, 8, 64), vmem(64, 8, 64),
        vmem(64, 128), vmem(64, 128), vmem(64, 128),
        vmem(512, 64), vmem(512, 64), vmem(512, 64), vmem(ng * 64, 64), vmem(ng * 64, 64),
        vmem(nx * 64, 64), vmem(nx * 64, 64), vmem(nz * 64, 64),
        vmem(512, 64), vmem(ng * 64, 128), vmem(nx * 64, 128), vmem(nz * 64, 64),
        vmem(ng, 32, 128), vmem(nx, 32, 128), vmem(nz, 32, 128),
        vmem(ng, 8, 128), vmem(nx, 8, 128), vmem(nz, 8, 128),
        vmem(5, 2, 8, 128), vmem(5, 2, 8, 128),
        dma(10), dma(3, top), dma(3, top), dma(3, top), dma(3, top), dma(5, 2), dma(5, 2),
    ]
    result, coarse = pl.pallas_call(
        functools.partial(kernel, nz, nx, ng),
        out_shape=(
            jax.ShapeDtypeStruct((64, 128), F32),
            jax.ShapeDtypeStruct((8, 64), F32),
        ),
        in_specs=[pl.BlockSpec(memory_space=pl.ANY)] * 8,
        out_specs=(
            pl.BlockSpec(memory_space=pltpu.VMEM),
            pl.BlockSpec(memory_space=pltpu.VMEM),
        ),
        scratch_shapes=scratch,
        compiler_params=pltpu.CompilerParams(
            collective_id=0, has_side_effects=True, vmem_limit_bytes=32 * 2**20
        ),
        name="v_cycle",
    )(
        right_side, fine_blocks, fine_inverse, pattern, tentative, slot_map,
        jnp.transpose(coarse_inverse, (0, 2, 1)), jnp.transpose(coarse_lower, (0, 2, 1)),
    )
    return result, coarse.T


def solution(mesh):
    slabs, ng = mesh.shape["slab"], mesh.shape["group"]
    nx = 4 if slabs % 4 == 0 and slabs > 4 else 2
    both = ("slab", "group")
    in_specs = (
        P(None, both), P(None, None, None, both), P(None, None, both), P(None, both), P(None, None, both),
        P(both, None), P(None, None, both), P(None, None, both),
    )
    return jax.shard_map(
        functools.partial(body, slabs // nx, nx, ng),
        mesh=mesh,
        in_specs=in_specs,
        out_specs=(P(None, both), P(None, both)),
        check_vma=False,
    )
```

time: 284 us -> 63.5 us (0.22)
  the two profiles are of different devices: /device:TPU:127 before, /device:TPU:1 now
where the time goes in v1:
time: 63.5 us; the launch traced here: 63.2 us
  Pallas kernels  52 us (82%)
  local copies, waits for them, and re-layouts  10.5 us (17%)
  between operations  0.66 us (1%)
    pallas_call x1, Pallas kernels, body(): pl.pallas_call(functools.partial(kernel, nz, nx, ng), out_shape=(jax.Shap...  52 us
    unnamed x18, local copies, waits for them, and re-layouts  10.5 us

profile of v1, /device:TPU:1, one launch (start us, length us, event | category | flops | bytes accessed | tf_op | source)
XLA Modules:
  0.0 63.2 jit_solution(13181595592339945963)
XLA Ops:
  0.6 0.0 copy-start
  0.6 2.8 %copy-done = f32[3,64,64,128]{3,2,1,0:T(8,128)S(1)} copy-done((f32[3,64,64,128]{3,2,1,0:T(8,128)S(1)}, f32[3,64,64,128]{3,2,1,0:T(8,128)}, u32[]{:S(2)}) %copy-start) | copy-done | bytes 6291480
  3.4 0.0 copy-start.1
  3.4 1.6 %copy-done.1 = f32[64,64,128]{2,1,0:T(8,128)S(1)} copy-done((f32[64,64,128]{2,1,0:T(8,128)S(1)}, f32[64,64,128]{2,1,0:T(8,128)}, u32[]{:S(2)}) %copy-start.1) | copy-done | bytes 2097176
  5.0 0.0 copy-start.2
  5.0 0.9 %copy-done.2 = f32[64,64,8]{1,2,0:T(8,128)S(1)} copy-done((f32[64,64,8]{1,2,0:T(8,128)S(1)}, f32[64,64,8]{1,2,0:T(8,128)}, u32[]{:S(2)}) %copy-start.2) | copy-done | bytes 131096
  6.0 0.0 copy-start.3
  6.0 0.9 %copy-done.3 = f32[64,64,8]{1,2,0:T(8,128)S(1)} copy-done((f32[64,64,8]{1,2,0:T(8,128)S(1)}, f32[64,64,8]{1,2,0:T(8,128)}, u32[]{:S(2)}) %copy-start.3) | copy-done | bytes 131096
  6.9 0.0 copy-start.4
  6.9 0.9 %copy-done.4 = f32[4,64,128]{2,1,0:T(8,128)S(1)} copy-done((f32[4,64,128]{2,1,0:T(8,128)S(1)}, f32[4,64,128]{2,1,0:T(8,128)}, u32[]{:S(2)}) %copy-start.4) | copy-done | bytes 131096
  7.8 0.0 copy-start.5
  7.8 0.8 %copy-done.5 = f32[64,128]{1,0:T(8,128)S(1)} copy-done((f32[64,128]{1,0:T(8,128)S(1)}, f32[64,128]{1,0:T(8,128)}, u32[]{:S(2)}) %copy-start.5) | copy-done | bytes 32792
  8.6 0.0 copy-start.6
  8.6 0.7 %copy-done.6 = s32[8,64]{1,0:T(8,128)S(1)} copy-done((s32[8,64]{1,0:T(8,128)S(1)}, s32[8,64]{1,0:T(8,128)}, u32[]{:S(2)}) %copy-start.6) | copy-done | bytes 2072
  9.3 0.0 copy-start.7
  9.3 0.7 %copy-done.7 = s32[2,128]{1,0:T(2,128)S(1)} copy-done((s32[2,128]{1,0:T(2,128)S(1)}, s32[2,128]{1,0:T(2,128)}, u32[]{:S(2)}) %copy-start.7) | copy-done | bytes 1048
  9.9 52.0 %v_cycle.1 = (f32[64,128]{1,0:T(8,128)S(1)}, f32[8,64]{1,0:T(8,128)S(1)}) custom-call(f32[64,128]{1,0:T(8,128)S(1)} %copy-done.5, f32[3,64,64,128]{3,2,1,0:T(8,128)S(1)} %copy-done, f32[64,64,128]{2,1,0:T(8,128)S(1)} %copy-done.1, s32[2,128]{1,0:T(2,128)S(1)} %copy-done.7, f32[4,64,128]{2,1,0:T(8,128)S(1)} %copy-done.4, s32[8,64]{1,0:T(8,128)S(1)} %copy-done.6, ...), custom_call_target="tpu_custom_call" | custom-call | tf_op jit(solution)/shard_map/v_cycle/pallas_call | solution.py:417
  62.0 0.6 copy.12
  62.6 0.6 copy.13
Async XLA Ops:
  0.6 2.8 %copy-start = (f32[3,64,64,128]{3,2,1,0:T(8,128)S(1)}, f32[3,64,64,128]{3,2,1,0:T(8,128)}, u32[]{:S(2)}) copy-start(f32[3,64,64,128]{3,2,1,0:T(8,128)} %f_h.1) | copy-start | bytes 18874372
  3.4 1.6 %copy-start.1 = (f32[64,64,128]{2,1,0:T(8,128)S(1)}, f32[64,64,128]{2,1,0:T(8,128)}, u32[]{:S(2)}) copy-start(f32[64,64,128]{2,1,0:T(8,128)} %i_h.1) | copy-start | bytes 6291460
  5.0 0.9 %copy-start.2 = (f32[64,64,8]{1,2,0:T(8,128)S(1)}, f32[64,64,8]{1,2,0:T(8,128)}, u32[]{:S(2)}) copy-start(f32[64,64,8]{1,2,0:T(8,128)} %param.14) | copy-start | bytes 393220
  6.0 0.9 %copy-start.3 = (f32[64,64,8]{1,2,0:T(8,128)S(1)}, f32[64,64,8]{1,2,0:T(8,128)}, u32[]{:S(2)}) copy-start(f32[64,64,8]{1,2,0:T(8,128)} %param.15) | copy-start | bytes 393220
  6.9 0.9 %copy-start.4 = (f32[4,64,128]{2,1,0:T(8,128)S(1)}, f32[4,64,128]{2,1,0:T(8,128)}, u32[]{:S(2)}) copy-start(f32[4,64,128]{2,1,0:T(8,128)} %tent_h.1) | copy-start | bytes 393220
  7.8 0.8 %copy-start.5 = (f32[64,128]{1,0:T(8,128)S(1)}, f32[64,128]{1,0:T(8,128)}, u32[]{:S(2)}) copy-start(f32[64,128]{1,0:T(8,128)} %b_h.1) | copy-start | bytes 98308
  8.6 0.7 %copy-start.6 = (s32[8,64]{1,0:T(8,128)S(1)}, s32[8,64]{1,0:T(8,128)}, u32[]{:S(2)}) copy-start(s32[8,64]{1,0:T(8,128)} %slot_h.1) | copy-start | bytes 6148
  9.3 0.7 %copy-start.7 = (s32[2,128]{1,0:T(2,128)S(1)}, s32[2,128]{1,0:T(2,128)}, u32[]{:S(2)}) copy-start(s32[2,128]{1,0:T(2,128)} %pat_h.1) | copy-start | bytes 3076

commit v2 on v1

--- a/solution.py
+++ b/solution.py
@@ -27,15 +27,40 @@
     return lax.dot_general(a, b, dims, preferred_element_type=F32)
 
 
-def dot3(a, b, dims=NN):
-    ah, al = split(a)
-    bh, bl = split(b)
-    return dot1(ah, bh, dims) + (dot1(ah, bl, dims) + dot1(al, bh, dims))
+def split3(x):
+    hi = x.astype(BF16)
+    rest = x - hi.astype(F32)
+    mid = rest.astype(BF16)
+    return hi, mid, (rest - mid.astype(F32)).astype(BF16)
+
+
+def halves(t):
+    n = t.shape[1] // 2
+    return t[:, :n] + t[:, n:]
+
+
+def dot4(a, b):
+    w = jnp.concatenate(split(b), axis=1)
+    if a.shape[0] < 64:
+        t = dot1(jnp.concatenate(split(a), axis=0), w)
+        return halves(t[: a.shape[0]] + t[a.shape[0] :])
+    return halves(dot1(jnp.concatenate(split(a), axis=1), jnp.concatenate([w, w], axis=0)))
+
+
+def dot4_nt(a, b):
+    t = dot1(jnp.concatenate(split(a), axis=0), jnp.concatenate(split(b), axis=0), NT)
+    return halves(t[: a.shape[0]] + t[a.shape[0] :])
+
+
+def dot9(a, b):
+    w = jnp.concatenate(split3(b), axis=1)
+    t = dot1(jnp.concatenate(split3(a), axis=1), jnp.concatenate([w] * 3, axis=0))
+    return t[:, :64] + (t[:, 64:128] + t[:, 128:])
 
 
 def dot2(a, b, dims=NN):
-    ah, al = split(a)
-    return dot1(ah, b, dims) + dot1(al, b, dims)
+    t = dot1(jnp.concatenate(split(a), axis=0), b, dims)
+    return t[: a.shape[0]] + t[a.shape[0] :]
 
 
 def iota(shape, dim):
@@ -83,13 +108,13 @@
     return jnp.concatenate([p[:, :64], p[:, 64:]], axis=0)
 
 
-def scan_products(ref, count):
+def scan_products(ref, count, dot=dot4):
     half = 1
     while half < count:
         for start in range(0, count, 2 * half):
             mid = start + half
             left = pl.ds(start * 64, half * 64)
-            ref[left, :] = dot3(ref[left, :], ref[pl.ds(mid * 64, 64), :])
+            ref[left, :] = dot(ref[left, :], ref[pl.ds(mid * 64, 64), :])
         half *= 2
 
 
@@ -99,7 +124,7 @@
         for start in range(0, count, 2 * half):
             mid = start + half
             right = pl.ds(mid * 64, half * 64)
-            ref[right, :] = dot3(ref[right, :], ref[pl.ds((mid - 1) * 64, 64), :])
+            ref[right, :] = dot4(ref[right, :], ref[pl.ds((mid - 1) * 64, 64), :])
         half *= 2
 
 
@@ -167,12 +192,12 @@
     for j in range(8):
         cij = ci[:, j, :]
         cis[pl.ds(j * 64, 64), :] = cij
-        m = -dot3(cij, cl[:, j, :])
+        m = -dot9(cij, cl[:, j, :])
         Pl[pl.ds(j * 64, 64), :] = m
         e = m.T
         Zl[pl.ds(j * 64, 64), :] = e
         Xl[pl.ds(j * 64, 64), :] = e
-    scan_products(Zl, 8)
+    scan_products(Zl, 8, dot9)
 
     pl.semaphore_wait(barrier, len(peers))
 
@@ -308,10 +333,11 @@
     upward(rm1, RM1, g, ng, m_recv.at[0], Z1, Zm1)
     RM2[x] = pack_matrix(Z1[0:64, :])
     rm2 = gather_start(RM2, x, along_x, nx, m_send.at[1], m_recv.at[1])
+    def weigh(ref, h, parts):
+        ref[pl.ds(h * 64, 64), :] = jnp.concatenate(split(jnp.concatenate(parts, axis=1)), axis=1)
+
     for h in range(ng):
-        W1[pl.ds(h * 64, 64), :] = jnp.concatenate(
-            [later(Z1, h, ng), jnp.where(h < g, later(Zm1, h, ng), 0.0)], axis=1
-        )
+        weigh(W1, h, [later(Z1, h, ng), jnp.where(h < g, later(Zm1, h, ng), 0.0)])
 
     fine_apply(1, work, h1, to_residue)
     tent_c.wait()
@@ -322,34 +348,29 @@
         values.append(row_sum(weight) * (1.0 / math.sqrt(64)))
     spread = jnp.where(own_block, jnp.concatenate(values, axis=1), 0.0)
     rhs = dot2(spread, GT, NT)
-    offsets = diagonal(dot3(rhs, cis[...], NT), 8)
+    offsets = diagonal(dot4_nt(rhs, cis[...]), 8)
     after_own = jnp.concatenate([Zl[64:512, :], eye], axis=0)
-    RV1[g] = padded(row_sum(dot3(offsets, after_own)))
+    RV1[g] = padded(row_sum(halves(dot2(offsets, jnp.concatenate(split(after_own), axis=1)))))
     rv1 = gather_start(RV1, g, in_group, ng, v_send.at[0], v_recv.at[0])
 
     upward(rm2, RM2, x, nx, m_recv.at[1], Z2, Zm2)
     RM3[z] = pack_matrix(Z2[0:64, :])
     rm3 = gather_start(RM3, z, along_z, nz, m_send.at[2], m_recv.at[2])
     for h in range(nx):
-        W2[pl.ds(h * 64, 64), :] = jnp.concatenate(
-            [later(Z2, h, nx), jnp.where(h < x, later(Zm2, h, nx), 0.0)], axis=1
-        )
+        weigh(W2, h, [later(Z2, h, nx), jnp.where(h < x, later(Zm2, h, nx), 0.0)])
 
     own = lanes_folded(offsets)
     row8 = iota((8, 64), 0)
     carried = jnp.broadcast_to(own[0:1], (8, 64))
     local = carried
     for j in range(1, 8):
-        carried = dot3(carried, Xl[pl.ds(j * 64, 64), :]) + own[j : j + 1]
+        carried = dot4(carried, Xl[pl.ds(j * 64, 64), :]) + own[j : j + 1]
         local = jnp.where(row8 >= j, carried, local)
     scan_prefix(Pl, 8)
 
     def inflow(ref, weights, count):
-        total = None
-        for h in range(count):
-            term = dot3(ref[h][:, :64], weights[pl.ds(h * 64, 64), :])
-            total = term if total is None else total + term
-        return total
+        flat = [ref[h] + pltpu.roll(ref[h + 1], 64, 1) for h in range(0, count, 2)]
+        return halves(dot2(jnp.concatenate(flat, axis=1), weights[...]))
 
     gather_wait(rv1, RV1, g, ng, v_recv.at[0])
     flow1 = inflow(RV1, W1, ng)
@@ -358,20 +379,19 @@
 
     upward(rm3, RM3, z, nz, m_recv.at[2], None, Zm3)
     A1 = Zm1[0:64, :]
-    A21 = dot3(Zm2[0:64, :], A1)
+    A21 = dot4(Zm2[0:64, :], A1)
     for h in range(nz):
-        W3[pl.ds(h * 64, 64), :] = jnp.where(h < z, later(Zm3, h, nz), 0.0)
-    W3[...] = dot3(W3[...], A21)
+        weigh(W3, h, [dot4(jnp.where(h < z, later(Zm3, h, nz), 0.0), A21)])
 
     gather_wait(rv2, RV2, x, nx, v_recv.at[1])
     flow2 = inflow(RV2, W2, nx)
     RV3[z] = padded(flow2[:, :64])
     rv3 = gather_start(RV3, z, along_z, nz, v_send.at[2], v_recv.at[2])
-    nearer = dot3(flow2[:, 64:], A1) + flow1[:, 64:]
+    nearer = dot4(flow2[:, 64:], A1) + flow1[:, 64:]
     gather_wait(rv3, RV3, z, nz, v_recv.at[2])
     incoming = inflow(RV3, W3, nz) + nearer
 
-    coarse = local + lanes_folded(diagonal(dot3(incoming, Pl[...], NT), 8))
+    coarse = local + lanes_folded(diagonal(dot4_nt(incoming, Pl[...]), 8))
     ce_ref[...] = coarse
     weights = jnp.where(own_block, dot2(coarse, GT), 0.0)
     total = None
@@ -408,7 +428,8 @@
         vmem(64, 128), vmem(64, 128), vmem(64, 128),
         vmem(512, 64), vmem(512, 64), vmem(512, 64), vmem(ng * 64, 64), vmem(ng * 64, 64),
         vmem(nx * 64, 64), vmem(nx * 64, 64), vmem(nz * 64, 64),
-        vmem(512, 64), vmem(ng * 64, 128), vmem(nx * 64, 128), vmem(nz * 64, 64),
+        vmem(512, 64),
+        pltpu.VMEM((ng * 64, 256), BF16), pltpu.VMEM((nx * 64, 256), BF16), pltpu.VMEM((nz * 64, 128), BF16),
         vmem(ng, 32, 128), vmem(nx, 32, 128), vmem(nz, 32, 128),
         vmem(ng, 8, 128), vmem(nx, 8, 128), vmem(nz, 8, 128),
         vmem(5, 2, 8, 128), vmem(5, 2, 8, 128),
@@ -427,7 +448,7 @@
         ),
         scratch_shapes=scratch,
         compiler_params=pltpu.CompilerParams(
-            collective_id=0, has_side_effects=True, vmem_limit_bytes=32 * 2**20
+            collective_id=0, has_side_effects=True, vmem_limit_bytes=60 * 2**20
         ),
         name="v_cycle",
     )(

time: 63.5 us -> 56.3 us (0.89)
  local copies, waits for them, and re-layouts: 10.5 us -> 2.65 us
  Pallas kernels: 52 us -> 52.8 us
    unnamed x18 -> x2, local copies, waits for them, and re-layouts: 10.5 us -> 2.65 us
    pallas_call x1, Pallas kernels: 52 us -> 52.8 us  [body(): pl.pallas_call(functools.partial(kernel, nz, nx, ng), out_shape=(jax.Shap...]
where the time goes in v2:
time: 56.3 us; the launch traced here: 56.1 us
  Pallas kernels  52.8 us (94%)
  local copies, waits for them, and re-layouts  2.65 us (5%)
  between operations  0.64 us (1%)
    pallas_call x1, Pallas kernels, body(): pl.pallas_call(functools.partial(kernel, nz, nx, ng), out_shape=(jax.Shap...  52.8 us
    unnamed x2, local copies, waits for them, and re-layouts  2.65 us

profile of v2, /device:TPU:1, one launch (start us, length us, event | category | flops | bytes accessed | tf_op | source)
XLA Modules:
  0.0 56.1 jit_solution(1509726734213349198)
XLA Ops:
  0.6 52.8 %v_cycle.1 = (f32[64,128]{1,0:T(8,128)}, f32[8,64]{1,0:T(8,128)}) custom-call(f32[64,128]{1,0:T(8,128)} %b_h.1, f32[3,64,64,128]{3,2,1,0:T(8,128)} %f_h.1, f32[64,64,128]{2,1,0:T(8,128)} %i_h.1, s32[2,128]{1,0:T(2,128)} %pat_h.1, f32[4,64,128]{2,1,0:T(8,128)} %tent_h.1, s32[8,64]{1,0:T(8,128)} %slot_h.1, f32[64,8,64]{2,1,0:T(8,128)} %bitcast.3, ...), custom_call_target="tpu_custom_call" | custom-call | tf_op jit(solution)/shard_map/v_cycle/pallas_call | solution.py:438
  53.5 1.4 %copy.12 = f32[64,128]{1,0:T(8,128)} copy(f32[64,128]{1,0:T(8,128)} %get-tuple-element.8) | data formatting | bytes 65536
  54.9 1.3 %copy.13 = f32[64,8]{0,1:T(8,128)} copy(f32[64,8]{0,1:T(8,128)} %bitcast.5) | data formatting | bytes 4096
